TPU v7x, 32 devices: a whole 2x2x4 slice. The times are simulated.
32 devices in a mesh: sub: 8 (over y, x, core), coarse: 4 (over z).
Axes of the slice: x: 2, y: 2, z: 4, core: 2. Of those that a mesh axis runs over, the one named last changes fastest.
Arguments:
- deflation: float32 [8, 64, 64, 512], P('sub', None, 'coarse')
- conductivity: float32 [8, 64, 512], P('sub', 'coarse'), may hold values from 0.1 to 10
- storage: float32 [8, 64, 512], P('sub', 'coarse'), may hold values from 0.5 to 4
- interface_rows: int32 [8, 4, 8, 512], P('sub', 'coarse'), may hold values from 0 to 8191, as said below
- interface_counts: int32 [8, 4, 8], P('sub', 'coarse'), may hold values from 0 to 512, as said below
Outputs:
- coarse_factor: float32 [8, 256, 256], P('sub')
- panel_rows: float32 [8, 4, 256, 512], P('sub', 'coarse')
Inputs may be any that keep to these rules, and one draw needn't show every extreme that they name: Slot j of a subdomain names the column offset o = j - 4 for j < 4 and j - 3 otherwise; interface_counts[a, c, slot of o] equals interface_counts[a + o, c, slot of -o], and is 0 where a + o lies outside 0 to 7. The most, 512, is reached in every draw. `interface_rows`: slots j < 4 hold cells with x = 0, the others cells with x = 15. Entries past a slot's count are also such cells and carry no edge.
All inputs are finite; a program needn't handle non-finite values.
Results may differ from a plain program's by a relative error of at most 0.0003.
Values sent between devices are 32-bit elements; how exact they have to be, the bound alone decides.
A program may use at most 64 MiB of HBM per device.

v0:
```python
import functools

import jax
import jax.numpy as jnp
from jax import lax
from jax.experimental import pallas as pl
from jax.experimental.pallas import tpu as pltpu
from jax.sharding import PartitionSpec as P

K = 64
CX = 16
REACH = 4
LANES = 128
SUB = 8
SLOTS = 2 * REACH
MESH = pl.DeviceIdType.MESH


def harmonic(first, second):
    return 2.0 * first * second / (first + second)


def offset_of(slot):
    return slot - REACH if slot < REACH else slot - REACH + 1


def halves(x):
    high = x.astype(jnp.bfloat16).astype(jnp.float32)
    return high, x - high


def split(x):
    return jnp.concatenate(halves(x), axis=0).astype(jnp.bfloat16)


def dot_nn(left, right):
    return lax.dot_general(left, right, (((1,), (0,)), ((), ())), preferred_element_type=jnp.float32)


def dot_nt(left, right):
    return lax.dot_general(left, right, (((1,), (1,)), ((), ())), preferred_element_type=jnp.float32)


def quad(g, at=0):
    return (g[:K, at : at + K] + g[K:, at : at + K]) + (g[:K, at + K : at + 2 * K] + g[K:, at + K : at + 2 * K])


def couple_kernel(
    n_sub, groups, layers, width,
    z_hbm, sig_hbm, sto_hbm, rows_hbm, cnt_hbm,
    bands_ref, lat_ref,
    z_ref, load_sem, sig_ref, sto_ref, rows_ref, cnt_ref, small_sem, sel_ref, lhs_ref, coef_ref, out_ref, in_ref, psig_out, psig_in, lay_out, lay_in, sig_out, sig_in,
    ret_out, ret_in, blk_ref, wgt_ref, hot_ref, own_band,
    send_sem, recv_sem, psig_send, psig_recv, lay_send, lay_recv, ret_send, ret_recv, band_send, band_recv,
):
    me = lax.axis_index("sub")
    level = lax.axis_index("coarse")
    cy = width // CX
    per = LANES // cy
    pad = rows_ref.shape[1]
    faces = cy * layers

    def load(c):
        return pltpu.make_async_copy(
            z_hbm.at[:, pl.ds(c * LANES, LANES)], z_ref.at[pl.ds(c * K * layers, K * layers)], load_sem.at[c]
        )

    small = [
        pltpu.make_async_copy(src, dst, small_sem.at[i])
        for i, (src, dst) in enumerate(
            ((sig_hbm, sig_ref), (rows_hbm, rows_ref), (sto_hbm, sto_ref), (cnt_hbm, cnt_ref))
        )
    ]
    for copy in small:
        copy.start()
    for c in range(width // LANES):
        load(c).start()

    def layer(z):
        return jnp.concatenate(
            [z_ref[pl.ds(c * K * layers + z, K, stride=layers), :] for c in range(width // LANES)], axis=1
        )

    def reachable(slot):
        other = me + offset_of(slot)
        return jnp.logical_and(other >= 0, other < n_sub)

    barrier = pltpu.get_barrier_semaphore()
    for slot in range(SLOTS):
        @pl.when(reachable(slot))
        def _():
            pl.semaphore_signal(barrier, inc=1, device_id={"sub": me + offset_of(slot)}, device_id_type=MESH)
    for step in range(1, groups):
        pl.semaphore_signal(
            barrier, inc=1, device_id={"coarse": lax.rem(level + step, groups)}, device_id_type=MESH
        )

    row = lax.broadcasted_iota(jnp.int32, (width, 2 * LANES), 0)
    lane = lax.broadcasted_iota(jnp.int32, (width, 2 * LANES), 1)
    cell = (lane % cy) * CX + jnp.where(lane >= LANES, CX - 1, 0)
    hit = row == cell
    part = (lane % LANES) // cy
    for i in range(per):
        sel_ref[i] = jnp.where(jnp.logical_and(hit, part == i), 1.0, 0.0).astype(jnp.bfloat16)

    for copy in small:
        copy.wait()
    sigma = sig_ref[...]
    sigma_split = split(sigma)
    placed = []
    for i in range(per):
        t = dot_nn(sigma_split, sel_ref[i])
        placed.append(t[:layers] + t[layers:])
    position = lax.broadcasted_iota(jnp.int32, (layers, width), 1)
    depth = lax.broadcasted_iota(jnp.int32, (layers, width), 0)
    wx = jnp.where(position % CX == CX - 1, 0.0, harmonic(sigma, pltpu.roll(sigma, width - 1, 1)))
    wy = jnp.where(position >= width - CX, 0.0, harmonic(sigma, pltpu.roll(sigma, width - CX, 1)))
    wz = jnp.where(depth == layers - 1, 0.0, harmonic(sigma, pltpu.roll(sigma, layers - 1, 0)))
    coef_ref[0] = 0.5 * (
        sto_ref[...] + (wx + pltpu.roll(wx, 1, 1)) + (wy + pltpu.roll(wy, CX, 1)) + (wz + pltpu.roll(wz, 1, 0))
    )
    coef_ref[1] = wx
    coef_ref[2] = wy
    coef_ref[3] = wz

    face_cell = lax.broadcasted_iota(jnp.int32, (faces, pad), 0)

    def onehot(slot):
        index = lax.shift_right_logical(rows_ref[slot : slot + 1, :], CX.bit_length() - 1)
        return jnp.where(face_cell == index, 1.0, 0.0).astype(jnp.bfloat16)

    for slot in range(1, SLOTS, 2):
        hot_ref[slot // 2] = onehot(slot)
    for c in range(width // LANES):
        load(c).wait()
    for g in range(layers // per):
        total = jnp.zeros((2 * K, 2 * LANES), jnp.float32)
        sig_row = jnp.zeros((1, 2 * LANES), jnp.float32)
        for i in range(per):
            z = g * per + i
            total = total + dot_nn(split(layer(z)), sel_ref[i])
            sig_row = sig_row + placed[i][z : z + 1]
        high, low = halves(sig_row)
        sig_rows = jnp.concatenate(
            [jnp.broadcast_to(high, (SUB, 2 * LANES)), jnp.broadcast_to(low, (SUB, 2 * LANES))], axis=0
        )
        stacked = jnp.concatenate([total, sig_rows], axis=0).astype(jnp.bfloat16)
        for f in range(2):
            lhs_ref[f, :, g * LANES : (g + 1) * LANES] = stacked[:, f * LANES : (f + 1) * LANES]

    lay_out[:K] = layer(0)
    lay_out[K:] = jnp.broadcast_to(sigma[:1], (SUB, width))
    sig_out[...] = jnp.broadcast_to(sigma[layers - 1 :], (SUB, width))

    beside = jnp.minimum(me, REACH) + jnp.minimum(n_sub - 1 - me, REACH)
    pl.semaphore_wait(barrier, beside + groups - 1)

    def down():
        return pltpu.make_async_remote_copy(
            src_ref=lay_out, dst_ref=lay_in, send_sem=lay_send.at[0], recv_sem=lay_recv.at[0],
            device_id={"coarse": level - 1}, device_id_type=MESH,
        )

    def up():
        return pltpu.make_async_remote_copy(
            src_ref=sig_out, dst_ref=sig_in, send_sem=lay_send.at[1], recv_sem=lay_recv.at[1],
            device_id={"coarse": level + 1}, device_id_type=MESH,
        )

    @pl.when(level > 0)
    def _():
        down().start()

    @pl.when(level < groups - 1)
    def _():
        up().start()

    def picked_copy(slot):
        mirror = SLOTS - 1 - slot
        return pltpu.make_async_remote_copy(
            src_ref=out_ref.at[slot], dst_ref=in_ref.at[mirror // 2],
            send_sem=send_sem.at[slot // 2], recv_sem=recv_sem.at[mirror // 2],
            device_id={"sub": me + offset_of(slot)}, device_id_type=MESH,
        )

    def sigma_copy(slot):
        mirror = SLOTS - 1 - slot
        return pltpu.make_async_remote_copy(
            src_ref=psig_out.at[slot], dst_ref=psig_in.at[mirror],
            send_sem=psig_send.at[slot], recv_sem=psig_recv.at[mirror],
            device_id={"sub": me + offset_of(slot)}, device_id_type=MESH,
        )

    for batch in ((1, 7), (3, 5), (0, 2, 4, 6)):
        for slot in batch:
            hot = hot_ref[slot // 2] if slot % 2 else onehot(slot)
            picked = dot_nn(lhs_ref[0 if slot < REACH else 1], hot)
            out_ref[slot] = picked[:K] + picked[K : 2 * K]
            psig_out[slot] = picked[2 * K : 2 * K + SUB] + picked[2 * K + SUB :]
        for slot in batch:
            @pl.when(reachable(slot))
            def _():
                if slot % 2:
                    picked_copy(slot).start()
                sigma_copy(slot).start()

    def some_layers(step, gram):
        start = step * per
        cells = [layer(start + i) for i in range(per)]
        cells.append(layer(min(start + per, layers - 1)))
        lefts, rights = [], []
        for i in range(per):
            z = start + i
            here = cells[i]
            applied = (
                coef_ref[0, z : z + 1, :] * here
                - coef_ref[1, z : z + 1, :] * pltpu.roll(here, width - 1, 1)
                - coef_ref[2, z : z + 1, :] * pltpu.roll(here, width - CX, 1)
                - coef_ref[3, z : z + 1, :] * cells[i + 1]
            )
            lefts.append(split(here))
            rights.append(split(applied))
        return gram + dot_nt(jnp.concatenate(lefts, axis=1), jnp.concatenate(rights, axis=1))

    gram = jnp.zeros((2 * K, 2 * K), jnp.float32)
    for step in range(layers // per):
        gram = some_layers(step, gram)
    half = quad(gram)
    own = half + half.T

    @pl.when(level < groups - 1)
    def _():
        down().wait_recv()

    @pl.when(level > 0)
    def _():
        up().wait_recv()

    for slot in range(SLOTS):
        @pl.when(reachable(slot))
        def _():
            sigma_copy(SLOTS - 1 - slot).wait_recv()

    has_above = level < groups - 1
    has_below = level > 0
    top = layer(layers - 1)
    bottom = layer(0)
    above = jnp.where(has_above, lay_in[:K], 0.0)
    upper = jnp.where(has_above, harmonic(sigma[layers - 1 :], lay_in[K : K + 1]), 0.0)
    lower = jnp.where(has_below, harmonic(sigma[:1], sig_in[:1]), 0.0)
    top_weighted = split(top * upper)
    upper_block = -quad(dot_nt(top_weighted, split(above)))
    spot = lax.broadcasted_iota(jnp.int32, (1, pad), 1)
    lefts = [top_weighted, split(bottom * lower)]
    rights = [split(top), split(bottom)]
    for slot in range(SLOTS):
        live = jnp.logical_and(spot < cnt_ref[0, 0, slot], reachable(slot))
        weight = jnp.where(live, harmonic(psig_out[slot, :1], psig_in[slot, :1]), 0.0)
        rows = out_ref[slot]
        lefts.append(split(rows * weight))
        rights.append(split(rows))
        if slot % 2 == 0:
            wgt_ref[slot // 2] = lefts[-1]
    own = own + quad(dot_nt(jnp.concatenate(lefts, axis=1), jnp.concatenate(rights, axis=1)))

    band = jnp.concatenate([own, upper_block], axis=1)
    own_band[...] = band

    def band_copy(step):
        return pltpu.make_async_remote_copy(
            src_ref=own_band, dst_ref=bands_ref.at[level],
            send_sem=band_send.at[step], recv_sem=band_recv.at[level],
            device_id={"coarse": lax.rem(level + step, groups)}, device_id_type=MESH,
        )

    for step in range(1, groups):
        band_copy(step).start()
    bands_ref[level] = band

    def ret_copy(slot):
        return pltpu.make_async_remote_copy(
            src_ref=ret_out.at[slot], dst_ref=ret_in.at[SLOTS - 1 - slot],
            send_sem=ret_send.at[slot], recv_sem=ret_recv.at[SLOTS - 1 - slot],
            device_id={"sub": me + offset_of(slot)}, device_id_type=MESH,
        )

    def ret_arrival(slot):
        return pltpu.make_async_remote_copy(
            src_ref=ret_out.at[SLOTS - 1 - slot], dst_ref=ret_in.at[slot],
            send_sem=ret_send.at[SLOTS - 1 - slot], recv_sem=ret_recv.at[slot],
            device_id={"sub": me + offset_of(slot)}, device_id_type=MESH,
        )

    for slot in range(0, SLOTS, 2):
        @pl.when(reachable(slot))
        def _():
            picked_copy(SLOTS - 1 - slot).wait_recv()

    wide = jnp.zeros((K, LANES - K), jnp.float32)
    for slot in range(0, SLOTS, 2):
        partner = jnp.where(reachable(slot), in_ref[slot // 2], 0.0)
        block = -quad(dot_nt(wgt_ref[slot // 2], split(partner)))
        blk_ref[slot] = block
        ret_out[slot] = jnp.concatenate([block.T, wide], axis=1)
    for slot in range(0, SLOTS, 2):
        @pl.when(reachable(slot))
        def _():
            ret_copy(slot).start()

    for slot in range(SLOTS):
        if slot % 2:
            @pl.when(reachable(slot))
            def _():
                ret_arrival(slot).wait_recv()

            blk_ref[slot] = jnp.where(reachable(slot), ret_in[slot, :, :K], 0.0)
    for pair in range(SLOTS // 2):
        lat_ref[:, pair * 2 * K : (pair + 1) * 2 * K] = jnp.concatenate(
            [blk_ref[2 * pair], blk_ref[2 * pair + 1]], axis=1
        )
    for step in range(1, groups):
        source = lax.rem(level + groups - step, groups)
        pltpu.make_async_remote_copy(
            src_ref=own_band, dst_ref=bands_ref.at[source],
            send_sem=band_send.at[step], recv_sem=band_recv.at[source],
            device_id={"coarse": source}, device_id_type=MESH,
        ).wait_recv()
    for step in range(1, groups):
        band_copy(step).wait_send()
    for slot in range(SLOTS):
        @pl.when(reachable(slot))
        def _():
            sigma_copy(slot).wait_send()
            if slot % 2:
                picked_copy(slot).wait_send()
            else:
                ret_copy(slot).wait_send()

    @pl.when(level > 0)
    def _():
        down().wait_send()

    @pl.when(level < groups - 1)
    def _():
        up().wait_send()


def spread(x, at):
    return jnp.broadcast_to(x[at : at + 1, :], x.shape)


def column(x, at):
    return jnp.broadcast_to(x[:, at : at + 1], (x.shape[0], LANES))


def eliminate(left, right):
    left, right = list(left), list(right)
    below = lax.broadcasted_iota(jnp.int32, (SUB, LANES), 0)
    for p in range(K // SUB):
        cols = [[column(left[g], p * SUB + j) for j in range(SUB)] for g in range(p, K // SUB)]
        head = cols[0]
        a, b = left[p], right[p]
        inverses, above, rows_a, rows_b, roots = [], [], [], [], []
        for j in range(0, SUB, 2):
            first, cross, second = spread(head[j], j), spread(head[j + 1], j), spread(head[j + 1], j + 1)
            inverse_1 = 1.0 / first
            inverse_2 = first * (1.0 / (first * second - cross * cross))
            ratio = cross * inverse_1
            scale_1 = jnp.where(below > j, head[j], 0.0) * inverse_1
            scale_2 = jnp.where(below > j + 1, head[j + 1] - scale_1 * cross, 0.0) * inverse_2

            def pair(x):
                top = spread(x, j)
                return top, spread(x, j + 1) - ratio * top

            entries_1, entries_2 = {j + 1: cross}, {}
            for k in range(j + 2, SUB):
                entries_1[k], entries_2[k] = pair(head[k])
                head[k] = (head[k] - scale_1 * entries_1[k]) - scale_2 * entries_2[k]
            inverses += [inverse_1, inverse_2]
            roots += [lax.rsqrt(first), lax.rsqrt(second - ratio * cross)]
            above += [entries_1, entries_2]
            top_a, next_a = pair(a)
            top_b, next_b = pair(b)
            a = (a - scale_1 * top_a) - scale_2 * next_a
            b = (b - scale_1 * top_b) - scale_2 * next_b
            rows_a += [top_a, next_a]
            rows_b += [top_b, next_b]
        left[p], right[p] = a, b
        for g in range(p + 1, K // SUB):
            tail = cols[g - p]
            la, lb = left[g], right[g]
            for j in range(SUB):
                scale = tail[j] * inverses[j]
                for k in range(j + 1, SUB):
                    tail[k] = tail[k] - scale * above[j][k]
                la = la - scale * rows_a[j]
                lb = lb - scale * rows_b[j]
            left[g], right[g] = la, lb
        for j in range(SUB):
            left[p] = jnp.where(below == j, left[p] * roots[j], left[p])
            right[p] = jnp.where(below == j, right[p] * roots[j], right[p])
    return left, right


def thirds(x):
    high, rest = halves(x)
    middle, low = halves(rest)
    return high, middle, low


def exact_tn(left, right):
    a, b, c = thirds(left)
    d, e, f = thirds(right)
    return lax.dot_general(
        jnp.concatenate([a, a, b, b, a, c], axis=0).astype(jnp.bfloat16),
        jnp.concatenate([d, e, d, e, f, d], axis=0).astype(jnp.bfloat16),
        (((0,), (0,)), ((), ())), preferred_element_type=jnp.float32,
    )


def factor_kernel(
    groups, bands_ref, lat_ref, factor_ref, panel_ref, low_ref, inv_ref, turn_ref, schur_ref, last_ref, scaled_ref, fit_ref
):
    level = lax.axis_index("coarse")
    row = lax.broadcasted_iota(jnp.int32, (K, LANES), 0)
    lane = lax.broadcasted_iota(jnp.int32, (K, LANES), 1)
    eye = jnp.where(row == lane, 1.0, 0.0)
    fit = []
    for k in range(groups):
        diagonal = jnp.where(row == lane, bands_ref[k], 0.0)
        fit.append((jnp.sum(diagonal, axis=0, keepdims=True)[:, :K], jnp.sum(diagonal, axis=1, keepdims=True)))
    for k in range(groups):
        after = fit[k + 1][0] if k + 1 < groups else jnp.ones((1, K), jnp.float32)
        along = jnp.concatenate([fit[k][0], after], axis=1)
        shrink = lax.rsqrt(along)
        scaled_ref[k] = bands_ref[k] * shrink * lax.rsqrt(fit[k][1])
        fit_ref[k, :1] = along * shrink
        fit_ref[k, 1:2] = shrink
    schur_ref[...] = jnp.zeros_like(schur_ref)
    last_ref[...] = jnp.zeros_like(last_ref)
    low_ref[0] = jnp.zeros_like(low_ref[0])
    inv_ref[0] = jnp.zeros_like(inv_ref[0])
    turn_ref[0] = jnp.zeros_like(turn_ref[0])

    def panel_block(k, before):
        right = jnp.where(level == k, lat_ref[...], 0.0) - exact_tn(turn_ref[before], last_ref[...])
        return exact_tn(inv_ref[jnp.maximum(k, 0)], right)

    def one_block(k, carry):
        done = jnp.maximum(k - 1, 0)
        last = panel_block(k - 1, jnp.maximum(k - 2, 0))
        start = scaled_ref[k] - schur_ref[...]
        tiles = [start[g * SUB : (g + 1) * SUB] for g in range(K // SUB)]
        ones = [eye[g * SUB : (g + 1) * SUB] for g in range(K // SUB)]
        left, right = eliminate(tiles, ones)
        left = jnp.concatenate(left, axis=0)
        right = jnp.concatenate(right, axis=0)
        left = jnp.where(lane >= row, left, 0.0)
        turn = left[:, K:]
        real_turn = (left * fit_ref[k, :1])[:, K:]
        last_ref[...] = last
        panel_ref[0, 0, pl.ds(pl.multiple_of(done * K, K), K), :] = last
        low_ref[k] = (left * fit_ref[k, :1]).T
        inv_ref[k] = (right * fit_ref[k, 1:2]).T[:K]
        turn_ref[k] = real_turn
        schur_ref[:, :K] = exact_tn(turn, turn)
        return carry

    factor_ref[0] = jnp.zeros_like(factor_ref[0])
    lax.fori_loop(0, groups, one_block, 0)
    panel_ref[0, 0, (groups - 1) * K :, :] = panel_block(groups - 1, groups - 2)
    for k in range(groups):
        factor_ref[0, k * K : (k + 1) * K, k * K : (k + 1) * K] = low_ref[k, :K]
        if k + 1 < groups:
            factor_ref[0, (k + 1) * K : (k + 2) * K, k * K : (k + 1) * K] = low_ref[k, K:]


def body(n_sub, groups, deflation, conductivity, storage, interface_rows, interface_counts):
    layers, width = deflation.shape[2], deflation.shape[3]
    pad = interface_rows.shape[3]
    faces = width // CX * layers
    f32 = jnp.float32
    vmem = pl.BlockSpec(memory_space=pltpu.VMEM)
    dma = pltpu.SemaphoreType.DMA
    bands, lateral = pl.pallas_call(
        functools.partial(couple_kernel, n_sub, groups, layers, width),
        out_shape=(
            jax.ShapeDtypeStruct((groups, K, 2 * K), f32),
            jax.ShapeDtypeStruct((K, SLOTS * K), f32),
        ),
        in_specs=[pl.BlockSpec(memory_space=pltpu.HBM)] * 5,
        out_specs=(vmem, vmem),
        scratch_shapes=[
            pltpu.VMEM((width // LANES * K * layers, LANES), f32),
            dma((width // LANES,)),
            pltpu.VMEM((layers, width), f32),
            pltpu.VMEM((layers, width), f32),
            pltpu.VMEM((SLOTS, pad), jnp.int32),
            pltpu.SMEM((1, 1, SLOTS), jnp.int32),
            dma((4,)),
            pltpu.VMEM((LANES * CX // width, width, 2 * LANES), jnp.bfloat16),
            pltpu.VMEM((2, 2 * K + 2 * SUB, faces), jnp.bfloat16),
            pltpu.VMEM((4, layers, width), f32),
            pltpu.VMEM((SLOTS, K, pad), f32),
            pltpu.VMEM((REACH, K, pad), f32),
            pltpu.VMEM((SLOTS, SUB, pad), f32),
            pltpu.VMEM((SLOTS, SUB, pad), f32),
            pltpu.VMEM((K + SUB, width), f32),
            pltpu.VMEM((K + SUB, width), f32),
            pltpu.VMEM((SUB, width), f32),
            pltpu.VMEM((SUB, width), f32),
            pltpu.VMEM((SLOTS, K, LANES), f32),
            pltpu.VMEM((SLOTS, K, LANES), f32),
            pltpu.VMEM((SLOTS, K, K), f32),
            pltpu.VMEM((REACH, 2 * K, pad), jnp.bfloat16),
            pltpu.VMEM((REACH, faces, pad), jnp.bfloat16),
            pltpu.VMEM((K, 2 * K), f32),
            dma((REACH,)), dma((REACH,)), dma((SLOTS,)), dma((SLOTS,)), dma((2,)), dma((2,)),
            dma((SLOTS,)), dma((SLOTS,)), dma((groups,)), dma((groups,)),
        ],
        compiler_params=pltpu.CompilerParams(
            collective_id=0, has_side_effects=True, vmem_limit_bytes=40 * 1024 * 1024
        ),
        name="couple",
    )(
        *(
            pltpu.with_memory_space_constraint(x, pltpu.HBM)
            for x in (
                deflation.reshape(K * layers, width), conductivity[0], storage[0],
                interface_rows[0, 0], interface_counts,
            )
        )
    )
    return pl.pallas_call(
        functools.partial(factor_kernel, groups),
        out_shape=(
            jax.ShapeDtypeStruct((1, groups * K, groups * K), f32),
            jax.ShapeDtypeStruct((1, 1, groups * K, SLOTS * K), f32),
        ),
        in_specs=[vmem, vmem],
        out_specs=(vmem, vmem),
        scratch_shapes=[
            pltpu.VMEM((groups, 2 * K, K), f32),
            pltpu.VMEM((groups, K, K), f32),
            pltpu.VMEM((groups, K, K), f32),
            pltpu.VMEM((K, LANES), f32),
            pltpu.VMEM((K, SLOTS * K), f32),
            pltpu.VMEM((groups, K, LANES), f32),
            pltpu.VMEM((groups, SUB, LANES), f32),
        ],
        compiler_params=pltpu.CompilerParams(vmem_limit_bytes=40 * 1024 * 1024),
        name="factor",
    )(bands, lateral)


def solution(mesh):
    placed = (
        P("sub", None, "coarse", None),
        P("sub", "coarse", None),
        P("sub", "coarse", None),
        P("sub", "coarse", None, None),
        P("sub", "coarse", None),
    )
    return jax.shard_map(
        functools.partial(body, mesh.shape["sub"], mesh.shape["coarse"]),
        mesh=mesh,
        in_specs=placed,
        out_specs=(P("sub", None, None), P("sub", "coarse", None, None)),
        check_vma=False,
    )
```

profile of v0, /device:TPU:0, one launch (start us, length us, event | category | flops | bytes accessed | tf_op | source)
XLA Modules:
  0.0 30.8 jit_solution(9093927050820763842)
XLA Ops:
  0.6 21.0 %couple.1 = (f32[4,64,128]{2,1,0:T(8,128)S(1)}, f32[64,512]{1,0:T(8,128)S(1)}) custom-call(f32[1024,512]{1,0:T(8,128)} %bitcast.4, f32[16,512]{1,0:T(8,128)} %bitcast.5, f32[16,512]{1,0:T(8,128)} %bitcast.6, s32[8,512]{1,0:T(8,128)} %bitcast.7, s32[1,1,8]{2,1,0:T(1,128)} %cnt_hbm.1), custom_call_target="tpu_custom_call" | custom-call | tf_op jit(solution)/shard_map/couple/pallas_call | solution.py:486
  21.7 9.1 %factor.1 = (f32[1,256,256]{2,1,0:T(8,128)}, f32[1,1,256,512]{3,2,1,0:T(8,128)}) custom-call(f32[4,64,128]{2,1,0:T(8,128)S(1)} %get-tuple-element.4.bands_ref, f32[64,512]{1,0:T(8,128)S(1)} %get-tuple-element.5.lat_ref), custom_call_target="tpu_custom_call" | custom-call | tf_op jit(solution)/shard_map/factor/pallas_call | solution.py:535
where the time goes:
time: 30.9 us; the launch traced here: 30.8 us
  Pallas kernels  30.1 us (97%)
  between operations  0.64 us (2%)
    pallas_call x1, Pallas kernels, body(): pl.pallas_call(functools.partial(couple_kernel, n_sub, groups, layers, wi...  21 us
    pallas_call x1, Pallas kernels, body(): pl.pallas_call(functools.partial(factor_kernel, groups), out_shape=(jax.S...  9.09 us

commit v1 on v0

--- a/solution.py
+++ b/solution.py
@@ -49,7 +49,7 @@
     n_sub, groups, layers, width,
     z_hbm, sig_hbm, sto_hbm, rows_hbm, cnt_hbm,
     bands_ref, lat_ref,
-    z_ref, load_sem, sig_ref, sto_ref, rows_ref, cnt_ref, small_sem, sel_ref, lhs_ref, coef_ref, out_ref, in_ref, psig_out, psig_in, lay_out, lay_in, sig_out, sig_in,
+    z_ref, flat_ref, cut_ref, pick_ref, load_sem, sig_ref, sto_ref, rows_ref, cnt_ref, small_sem, sel_ref, lhs_ref, coef_ref, out_ref, in_ref, psig_out, psig_in, lay_out, lay_in, sig_out, sig_in,
     ret_out, ret_in, blk_ref, wgt_ref, hot_ref, own_band,
     send_sem, recv_sem, psig_send, psig_recv, lay_send, lay_recv, ret_send, ret_recv, band_send, band_recv,
 ):
@@ -138,7 +138,11 @@
         sig_row = jnp.zeros((1, 2 * LANES), jnp.float32)
         for i in range(per):
             z = g * per + i
-            total = total + dot_nn(split(layer(z)), sel_ref[i])
+            here = layer(z)
+            flat_ref[z] = here
+            cut = split(here)
+            cut_ref[z] = cut
+            total = total + dot_nn(cut, sel_ref[i])
             sig_row = sig_row + placed[i][z : z + 1]
         high, low = halves(sig_row)
         sig_rows = jnp.concatenate(
@@ -148,7 +152,7 @@
         for f in range(2):
             lhs_ref[f, :, g * LANES : (g + 1) * LANES] = stacked[:, f * LANES : (f + 1) * LANES]
 
-    lay_out[:K] = layer(0)
+    lay_out[:K] = flat_ref[0]
     lay_out[K:] = jnp.broadcast_to(sigma[:1], (SUB, width))
     sig_out[...] = jnp.broadcast_to(sigma[layers - 1 :], (SUB, width))
 
@@ -196,6 +200,7 @@
             hot = hot_ref[slot // 2] if slot % 2 else onehot(slot)
             picked = dot_nn(lhs_ref[0 if slot < REACH else 1], hot)
             out_ref[slot] = picked[:K] + picked[K : 2 * K]
+            pick_ref[slot] = picked[: 2 * K].astype(jnp.bfloat16)
             psig_out[slot] = picked[2 * K : 2 * K + SUB] + picked[2 * K + SUB :]
         for slot in batch:
             @pl.when(reachable(slot))
@@ -206,25 +211,23 @@
 
     def some_layers(step, gram):
         start = step * per
-        cells = [layer(start + i) for i in range(per)]
-        cells.append(layer(min(start + per, layers - 1)))
+        cells = [flat_ref[start + i] for i in range(per)]
+        cells.append(flat_ref[jnp.minimum(start + per, layers - 1)])
         lefts, rights = [], []
         for i in range(per):
             z = start + i
             here = cells[i]
             applied = (
-                coef_ref[0, z : z + 1, :] * here
-                - coef_ref[1, z : z + 1, :] * pltpu.roll(here, width - 1, 1)
-                - coef_ref[2, z : z + 1, :] * pltpu.roll(here, width - CX, 1)
-                - coef_ref[3, z : z + 1, :] * cells[i + 1]
+                coef_ref[0, pl.ds(z, 1), :] * here
+                - coef_ref[1, pl.ds(z, 1), :] * pltpu.roll(here, width - 1, 1)
+                - coef_ref[2, pl.ds(z, 1), :] * pltpu.roll(here, width - CX, 1)
+                - coef_ref[3, pl.ds(z, 1), :] * cells[i + 1]
             )
-            lefts.append(split(here))
+            lefts.append(cut_ref[z])
             rights.append(split(applied))
         return gram + dot_nt(jnp.concatenate(lefts, axis=1), jnp.concatenate(rights, axis=1))
 
-    gram = jnp.zeros((2 * K, 2 * K), jnp.float32)
-    for step in range(layers // per):
-        gram = some_layers(step, gram)
+    gram = lax.fori_loop(0, layers // per, some_layers, jnp.zeros((2 * K, 2 * K), jnp.float32))
     half = quad(gram)
     own = half + half.T
 
@@ -243,8 +246,8 @@
 
     has_above = level < groups - 1
     has_below = level > 0
-    top = layer(layers - 1)
-    bottom = layer(0)
+    top = flat_ref[layers - 1]
+    bottom = flat_ref[0]
     above = jnp.where(has_above, lay_in[:K], 0.0)
     upper = jnp.where(has_above, harmonic(sigma[layers - 1 :], lay_in[K : K + 1]), 0.0)
     lower = jnp.where(has_below, harmonic(sigma[:1], sig_in[:1]), 0.0)
@@ -252,13 +255,13 @@
     upper_block = -quad(dot_nt(top_weighted, split(above)))
     spot = lax.broadcasted_iota(jnp.int32, (1, pad), 1)
     lefts = [top_weighted, split(bottom * lower)]
-    rights = [split(top), split(bottom)]
+    rights = [cut_ref[layers - 1], cut_ref[0]]
     for slot in range(SLOTS):
         live = jnp.logical_and(spot < cnt_ref[0, 0, slot], reachable(slot))
         weight = jnp.where(live, harmonic(psig_out[slot, :1], psig_in[slot, :1]), 0.0)
         rows = out_ref[slot]
         lefts.append(split(rows * weight))
-        rights.append(split(rows))
+        rights.append(pick_ref[slot])
         if slot % 2 == 0:
             wgt_ref[slot // 2] = lefts[-1]
     own = own + quad(dot_nt(jnp.concatenate(lefts, axis=1), jnp.concatenate(rights, axis=1)))
@@ -493,6 +496,9 @@
         out_specs=(vmem, vmem),
         scratch_shapes=[
             pltpu.VMEM((width // LANES * K * layers, LANES), f32),
+            pltpu.VMEM((layers, K, width), f32),
+            pltpu.VMEM((layers, 2 * K, width), jnp.bfloat16),
+            pltpu.VMEM((SLOTS, 2 * K, pad), jnp.bfloat16),
             dma((width // LANES,)),
             pltpu.VMEM((layers, width), f32),
             pltpu.VMEM((layers, width), f32),

time: 30.9 us -> 30.7 us (level)
  no operation moved by 1% of the time
where the time goes in v1:
time: 30.7 us; the launch traced here: 30.5 us
  Pallas kernels  29.9 us (97%)
  between operations  0.64 us (2%)
    pallas_call x1, Pallas kernels, body(): pl.pallas_call(functools.partial(couple_kernel, n_sub, groups, layers, wi...  20.8 us
    pallas_call x1, Pallas kernels, body(): pl.pallas_call(functools.partial(factor_kernel, groups), out_shape=(jax.S...  9.09 us

profile of v1, /device:TPU:0, one launch (start us, length us, event | category | flops | bytes accessed | tf_op | source)
XLA Modules:
  0.0 30.5 jit_solution(9768610188196450274)
XLA Ops:
  0.6 20.8 %couple.1 = (f32[4,64,128]{2,1,0:T(8,128)S(1)}, f32[64,512]{1,0:T(8,128)S(1)}) custom-call(f32[1024,512]{1,0:T(8,128)} %bitcast.4, f32[16,512]{1,0:T(8,128)} %bitcast.5, f32[16,512]{1,0:T(8,128)} %bitcast.6, s32[8,512]{1,0:T(8,128)} %bitcast.7, s32[1,1,8]{2,1,0:T(1,128)} %cnt_hbm.1), custom_call_target="tpu_custom_call" | custom-call | tf_op jit(solution)/shard_map/couple/pallas_call | solution.py:489
  21.4 9.1 %factor.1 = (f32[1,256,256]{2,1,0:T(8,128)}, f32[1,1,256,512]{3,2,1,0:T(8,128)}) custom-call(f32[4,64,128]{2,1,0:T(8,128)S(1)} %get-tuple-element.4.bands_ref, f32[64,512]{1,0:T(8,128)S(1)} %get-tuple-element.5.lat_ref), custom_call_target="tpu_custom_call" | custom-call | tf_op jit(solution)/shard_map/factor/pallas_call | solution.py:541
